TPU v7x, 256 devices: a whole 4x4x8 slice. The times are simulated.
256 devices in a mesh: ctx: 64 (over z, x_lo, y), kvh: 4 (over x_hi, core).
Axes of the slice: x: 4 (x_hi: 2, x_lo: 2; x = x_hi * 2 + x_lo), y: 4, z: 8, core: 2. Of those that a mesh axis runs over, the one named last changes fastest.
Arguments:
- queries: bfloat16 [16384, 64, 128], P('ctx', 'kvh'), may hold values from -16 to 16
- keys: bfloat16 [16384, 4, 128], P('ctx', 'kvh'), may hold values from -8 to 8
- values: bfloat16 [16384, 4, 128], P('ctx', 'kvh'), may hold values from -6 to 6
- doc_ids: int32 [16384], P('ctx'), may hold values from 0 to 127, never falling along the last dimension, each value on 1 to 768 neighbouring positions
Outputs:
- attended: bfloat16 [16384, 8192], P(('ctx', 'kvh'))
Inputs may be any that keep to these rules, and one draw needn't show every extreme that they name: doc_ids never falls along the sequence; every document has 1 to 768 positions and one has exactly 768.
All inputs are finite; a program needn't handle non-finite values.
Results may differ from a plain program's by a relative error of at most 0.0039.
Values may be sent and summed in bfloat16 or wider, within the bound.
A program may use at most 64 MiB of HBM per device.

v0:
```python
import jax
import jax.numpy as jnp
from jax import lax
from jax.sharding import PartitionSpec as P

STEPS = 4


def passed_along(value, axis, by):
    devices = lax.axis_size(axis)
    return lax.ppermute(value, axis, [(i, (i + by) % devices) for i in range(devices)])


def body(queries, keys, values, doc_ids):
    rows = queries.shape[0]
    heads_local = queries.shape[1]
    kv_local = keys.shape[1]
    width = queries.shape[2]
    group = heads_local // kv_local
    scale = 1.0 / width**0.5
    shards = lax.axis_size("ctx")
    myself = lax.axis_index("ctx")
    offsets = jnp.arange(rows, dtype=jnp.int32)
    grouped = queries.reshape(rows, kv_local, group, width)
    initial = (
        jnp.full((kv_local, group, rows), -jnp.inf, jnp.float32),
        jnp.zeros((kv_local, group, rows), jnp.float32),
        jnp.zeros((kv_local, group, rows, width), jnp.float32),
    )
    visitor = grouped
    visitor_ids = doc_ids
    state = initial
    for step in range(STEPS):
        query_shard = (myself + step) % shards
        query_block = visitor
        query_pos = query_shard * rows + offsets
        key_pos = myself * rows + offsets
        allowed = (visitor_ids[:, None] == doc_ids[None, :]) & (
            key_pos[None, :] <= query_pos[:, None]
        )
        update_top, update_total, update_summed = state
        score = (
            jnp.einsum("qhgd,khd->hgqk", query_block, keys, preferred_element_type=jnp.float32)
            * scale
        )
        score = jnp.where(allowed, score, -jnp.inf)
        new_top = jnp.maximum(update_top, jnp.max(score, axis=-1))
        factor = jnp.exp(update_top - new_top)
        weight = jnp.exp(score - new_top[..., None])
        new_total = update_total * factor + jnp.sum(weight, axis=-1)
        product = jnp.einsum(
            "hgqk,khd->hgqd",
            weight.astype(jnp.bfloat16),
            values,
            preferred_element_type=jnp.float32,
        )
        state = (new_top, new_total, update_summed * factor[..., None] + product)
        if step + 1 < STEPS:
            moved = passed_along(
                (
                    visitor.astype(jnp.float32),
                    visitor_ids.astype(jnp.float32),
                    state[0],
                    state[1],
                    state[2],
                ),
                "ctx",
                -1,
            )
            visitor = moved[0].astype(jnp.bfloat16)
            visitor_ids = moved[1].astype(jnp.int32)
            state = (moved[2], moved[3], moved[4])
    top, total, summed = state
    result = summed / total[..., None]
    finished = passed_along(
        result.transpose(2, 0, 1, 3).reshape(rows, heads_local * width).astype(jnp.bfloat16),
        "ctx",
        STEPS - 1,
    )
    return lax.all_to_all(finished, "kvh", split_axis=0, concat_axis=1, tiled=True)


def solution(mesh):
    return jax.shard_map(
        body,
        mesh=mesh,
        in_specs=(P("ctx", "kvh", None), P("ctx", "kvh", None), P("ctx", "kvh", None), P("ctx")),
        out_specs=P(("ctx", "kvh"), None),
        check_vma=False,
    )
```

profile of v0, /device:TPU:8, one launch (start us, length us, event | category | flops | bytes accessed | tf_op | source)
XLA Modules:
  0.0 299.4 jit_solution(3869024710721949256)
XLA Ops:
  0.0 0.0 copy-start
  0.0 0.0 copy-start.2
  0.0 0.7 convert_element_type.61
  0.7 2.2 collective-permute-start.2
  2.9 1.4 collective-permute-done.2
  4.3 7.4 %collective-permute-start.6 = (f32[256]{0:T(256)S(1)}, f32[256]{0:T(256)S(1)}, u32[]{:S(2)}, u32[]{:S(2)}) collective-permute-start(f32[256]{0:T(256)S(1)} %get-tuple-element.17), channel_id=1, source_target_pairs={{0,252},{4,0},{8,4},{12,8},{16,12},{20,16},{24,20},{28,24},{32,28}... | collective-permute-start | bytes 3080 | tf_op jit(solution)/shard_map/ppermute | solution.py:11
  11.7 1.3 collective-permute-done.6
  13.0 6.5 %collective-permute-start.10 = (f32[256]{0:T(256)S(1)}, f32[256]{0:T(256)S(1)}, u32[]{:S(2)}, u32[]{:S(2)}) collective-permute-start(f32[256]{0:T(256)S(1)} %get-tuple-element.15), channel_id=1, source_target_pairs={{0,252},{4,0},{8,4},{12,8},{16,12},{20,16},{24,20},{28,24},{32,28}... | collective-permute-start | bytes 3080 | tf_op jit(solution)/shard_map/ppermute | solution.py:11
  19.5 1.3 collective-permute-done.10
  20.8 1.0 compare_and_fusion
  21.8 0.0 copy-done
  21.9 2.0 fusion.8
  23.9 0.0 copy-start.1
  23.9 0.0 copy-done.2
  24.0 1.6 add_bitcast_fusion
  25.6 6.6 %collective-permute-start = (f32[1,16,256,128]{3,2,1,0:T(8,128)S(1)}, f32[1,16,256,128]{3,2,1,0:T(8,128)S(1)}, u32[]{:S(2)}, u32[]{:S(2)}) collective-permute-start(f32[1,16,256,128]{3,2,1,0:T(8,128)S(1)} %add_bitcast_fusion), channel_id=1, source_target_pairs={{0,252},{4,0},{8,4},{12,8},{16,12},{20,16},{24,20},{28,24},{32,28}... | collective-permute-start | bytes 6291464 | tf_op jit(solution)/shard_map/ppermute | solution.py:11
  32.1 0.0 copy-done.1
  32.1 0.3 copy.47
  32.4 6.5 %collective-permute-start.3 = (bf16[256,1,16,128]{3,0,2,1:T(8,128)(2,1)S(1)}, bf16[256,1,16,128]{3,0,2,1:T(8,128)(2,1)S(1)}, u32[]{:S(2)}, u32[]{:S(2)}) collective-permute-start(bf16[256,1,16,128]{3,0,2,1:T(8,128)(2,1)S(1)} %bitcast.194), channel_id=1, source_target_pairs={{0,252},{4,0},{8,4},{12,8},{16,12},{20,16},{24,20},{28,24},{32,28}... | collective-permute-start | bytes 3145736 | tf_op jit(solution)/shard_map/ppermute | solution.py:11
  39.0 0.1 collective-permute-start.1
  39.0 57.5 %collective-permute-done.3 = bf16[256,1,16,128]{3,0,2,1:T(8,128)(2,1)S(1)} collective-permute-done((bf16[256,1,16,128]{3,0,2,1:T(8,128)(2,1)S(1)}, bf16[256,1,16,128]{3,0,2,1:T(8,128)(2,1)S(1)}, u32[]{:S(2)}, u32[]{:S(2)}) %collective-permute-start.3) | collective-permute-done | bytes 1048608 | tf_op jit(solution)/shard_map/ppermute | solution.py:11
  96.5 0.7 fusion.9
  97.3 0.0 collective-permute-done.1
  97.3 0.0 collective-permute-done
  97.3 1.6 bitcast_add_fusion.2
  98.9 6.3 %collective-permute-start.4 = (f32[1,16,256,128]{3,2,1,0:T(8,128)S(1)}, f32[1,16,256,128]{3,2,1,0:T(8,128)S(1)}, u32[]{:S(2)}, u32[]{:S(2)}) collective-permute-start(f32[1,16,256,128]{3,2,1,0:T(8,128)S(1)} %bitcast_add_fusion.2), channel_id=1, source_target_pairs={{0,252},{4,0},{8,4},{12,8},{16,12},{20,16},{24,20},{28,24},{32,28}... | collective-permute-start | bytes 6291464 | tf_op jit(solution)/shard_map/ppermute | solution.py:11
  105.2 6.7 %collective-permute-start.7 = (bf16[256,1,16,128]{3,0,2,1:T(8,128)(2,1)S(1)}, bf16[256,1,16,128]{3,0,2,1:T(8,128)(2,1)S(1)}, u32[]{:S(2)}, u32[]{:S(2)}) collective-permute-start(bf16[256,1,16,128]{3,0,2,1:T(8,128)(2,1)S(1)} %collective-permute-done.3), channel_id=1, source_target_pairs={{0,252},{4,0},{8,4},{12,8},{16,12},{20,16},{24,20},{28,24},{32,28}... | collective-permute-start | bytes 3145736 | tf_op jit(solution)/shard_map/ppermute | solution.py:11
  111.9 0.9 fusion
  112.8 0.2 collective-permute-start.12
  113.0 0.3 collective-permute-start.5
  113.2 55.2 %collective-permute-done.7 = bf16[256,1,16,128]{3,0,2,1:T(8,128)(2,1)S(1)} collective-permute-done((bf16[256,1,16,128]{3,0,2,1:T(8,128)(2,1)S(1)}, bf16[256,1,16,128]{3,0,2,1:T(8,128)(2,1)S(1)}, u32[]{:S(2)}, u32[]{:S(2)}) %collective-permute-start.7) | collective-permute-done | bytes 1048608 | tf_op jit(solution)/shard_map/ppermute | solution.py:11
  168.4 6.7 %collective-permute-start.11 = (bf16[256,1,16,128]{3,0,2,1:T(8,128)(2,1)S(1)}, bf16[256,1,16,128]{3,0,2,1:T(8,128)(2,1)S(1)}, u32[]{:S(2)}, u32[]{:S(2)}) collective-permute-start(bf16[256,1,16,128]{3,0,2,1:T(8,128)(2,1)S(1)} %collective-permute-done.7), channel_id=1, source_target_pairs={{0,252},{4,0},{8,4},{12,8},{16,12},{20,16},{24,20},{28,24},{32,28}... | collective-permute-start | bytes 3145736 | tf_op jit(solution)/shard_map/ppermute | solution.py:11
  175.1 0.7 fusion.10
  175.8 0.0 collective-permute-done.5
  175.8 0.0 collective-permute-done.4
  175.9 1.6 bitcast_add_fusion.1
  177.5 6.8 %collective-permute-start.8 = (f32[1,16,256,128]{3,2,1,0:T(8,128)S(1)}, f32[1,16,256,128]{3,2,1,0:T(8,128)S(1)}, u32[]{:S(2)}, u32[]{:S(2)}) collective-permute-start(f32[1,16,256,128]{3,2,1,0:T(8,128)S(1)} %bitcast_add_fusion.1), channel_id=1, source_target_pairs={{0,252},{4,0},{8,4},{12,8},{16,12},{20,16},{24,20},{28,24},{32,28}... | collective-permute-start | bytes 6291464 | tf_op jit(solution)/shard_map/ppermute | solution.py:11
  184.3 0.9 fusion.2
  185.1 0.0 collective-permute-done.12
  185.2 0.1 collective-permute-start.13
  185.3 0.9 fusion.4
  186.1 0.1 collective-permute-start.9
  186.2 51.0 %collective-permute-done.13 = f32[1,16,256]{2,1,0:T(8,128)S(1)} collective-permute-done((f32[1,16,256]{2,1,0:T(8,128)S(1)}, f32[1,16,256]{2,1,0:T(8,128)S(1)}, u32[]{:S(2)}, u32[]{:S(2)}) %collective-permute-start.13) | collective-permute-done | bytes 16416 | tf_op jit(solution)/shard_map/ppermute | solution.py:11
  237.3 6.8 %collective-permute-start.14 = (f32[1,16,256]{2,1,0:T(8,128)S(1)}, f32[1,16,256]{2,1,0:T(8,128)S(1)}, u32[]{:S(2)}, u32[]{:S(2)}) collective-permute-start(f32[1,16,256]{2,1,0:T(8,128)S(1)} %bitcast_add_fusion.4), channel_id=1, source_target_pairs={{0,252},{4,0},{8,4},{12,8},{16,12},{20,16},{24,20},{28,24},{32,28}... | collective-permute-start | bytes 49160 | tf_op jit(solution)/shard_map/ppermute | solution.py:11
  244.0 0.0 collective-permute-done.11
  244.0 0.7 fusion.11
  244.8 0.0 collective-permute-done.9
  244.8 0.9 fusion.6
  245.7 0.0 collective-permute-done.14
  245.7 0.0 collective-permute-done.8
  245.7 2.3 fusion.55
  248.0 0.5 copy.31
  248.6 0.1 collective-permute-start.15
  248.7 29.4 %collective-permute-done.15 = bf16[256,2048]{0,1:T(8,128)(2,1)S(1)} collective-permute-done((bf16[256,2048]{0,1:T(8,128)(2,1)S(1)}, bf16[256,2048]{0,1:T(8,128)(2,1)S(1)}, u32[]{:S(2)}, u32[]{:S(2)}) %collective-permute-start.15) | collective-permute-done | bytes 1048608 | tf_op jit(solution)/shard_map/ppermute | solution.py:11
  278.0 0.6 copy.32
  278.7 19.6 %all_to_all.19 = bf16[4,64,2048]{2,1,0:T(8,128)(2,1)S(1)} all-to-all(bf16[4,64,2048]{2,1,0:T(8,128)(2,1)S(1)} %bitcast.192), channel_id=1, replica_groups=mesh['ctx'=64,'kvh'=4] {'kvh'}, dimensions={0} | all-to-all | bytes 2097152 | tf_op jit(solution)/shard_map/all_to_all | solution.py:80
  298.3 1.0 copy.41
  (14 shorter events, 0.1 us)
Async XLA Ops:
  0.0 21.9 %copy-start = (bf16[256,1,128]{2,0,1:T(8,128)(2,1)S(1)}, bf16[256,1,128]{2,0,1:T(8,128)(2,1)}, u32[]{:S(2)}) copy-start(bf16[256,1,128]{2,0,1:T(8,128)(2,1)} %param.5) | copy-start | bytes 196612
  0.0 23.9 %copy-start.2 = (bf16[256,1,128]{2,0,1:T(8,128)(2,1)S(1)}, bf16[256,1,128]{2,0,1:T(8,128)(2,1)}, u32[]{:S(2)}) copy-start(bf16[256,1,128]{2,0,1:T(8,128)(2,1)} %param.6) | copy-start | bytes 196612
  0.7 3.6 %collective-permute-start.2 = (f32[256]{0:T(256)S(1)}, f32[256]{0:T(256)S(1)}, u32[]{:S(2)}, u32[]{:S(2)}) collective-permute-start(f32[256]{0:T(256)S(1)} %convert_element_type.61), channel_id=1, source_target_pairs={{0,252},{4,0},{8,4},{12,8},{16,12},{20,16},{24,20},{28,24},{32,28}... | collective-permute-start | bytes 3080 | tf_op jit(solution)/shard_map/ppermute | solution.py:11
  4.3 8.7 %collective-permute-start.6 = (f32[256]{0:T(256)S(1)}, f32[256]{0:T(256)S(1)}, u32[]{:S(2)}, u32[]{:S(2)}) collective-permute-start(f32[256]{0:T(256)S(1)} %get-tuple-element.17), channel_id=1, source_target_pairs={{0,252},{4,0},{8,4},{12,8},{16,12},{20,16},{24,20},{28,24},{32,28}... | collective-permute-start | bytes 3080 | tf_op jit(solution)/shard_map/ppermute | solution.py:11
  13.0 7.8 %collective-permute-start.10 = (f32[256]{0:T(256)S(1)}, f32[256]{0:T(256)S(1)}, u32[]{:S(2)}, u32[]{:S(2)}) collective-permute-start(f32[256]{0:T(256)S(1)} %get-tuple-element.15), channel_id=1, source_target_pairs={{0,252},{4,0},{8,4},{12,8},{16,12},{20,16},{24,20},{28,24},{32,28}... | collective-permute-start | bytes 3080 | tf_op jit(solution)/shard_map/ppermute | solution.py:11
  23.9 8.2 %copy-start.1 = (bf16[256,16,128]{2,1,0:T(8,128)(2,1)S(1)}, bf16[256,16,128]{2,1,0:T(8,128)(2,1)}, u32[]{:S(2)}) copy-start(bf16[256,16,128]{2,1,0:T(8,128)(2,1)} %param.4) | copy-start | bytes 3145732
  25.6 71.7 %collective-permute-start = (f32[1,16,256,128]{3,2,1,0:T(8,128)S(1)}, f32[1,16,256,128]{3,2,1,0:T(8,128)S(1)}, u32[]{:S(2)}, u32[]{:S(2)}) collective-permute-start(f32[1,16,256,128]{3,2,1,0:T(8,128)S(1)} %add_bitcast_fusion), channel_id=1, source_target_pairs={{0,252},{4,0},{8,4},{12,8},{16,12},{20,16},{24,20},{28,24},{32,28}... | collective-permute-start | bytes 6291464 | tf_op jit(solution)/shard_map/ppermute | solution.py:11
  32.4 64.1 %collective-permute-start.3 = (bf16[256,1,16,128]{3,0,2,1:T(8,128)(2,1)S(1)}, bf16[256,1,16,128]{3,0,2,1:T(8,128)(2,1)S(1)}, u32[]{:S(2)}, u32[]{:S(2)}) collective-permute-start(bf16[256,1,16,128]{3,0,2,1:T(8,128)(2,1)S(1)} %bitcast.194), channel_id=1, source_target_pairs={{0,252},{4,0},{8,4},{12,8},{16,12},{20,16},{24,20},{28,24},{32,28}... | collective-permute-start | bytes 3145736 | tf_op jit(solution)/shard_map/ppermute | solution.py:11
  39.0 58.3 %collective-permute-start.1 = (f32[1,16,256]{2,1,0:T(8,128)S(1)}, f32[1,16,256]{2,1,0:T(8,128)S(1)}, u32[]{:S(2)}, u32[]{:S(2)}) collective-permute-start(f32[1,16,256]{2,1,0:T(8,128)S(1)} %bitcast.196), channel_id=1, source_target_pairs={{0,252},{4,0},{8,4},{12,8},{16,12},{20,16},{24,20},{28,24},{32,28}... | collective-permute-start | bytes 49160 | tf_op jit(solution)/shard_map/ppermute | solution.py:11
  98.9 76.9 %collective-permute-start.4 = (f32[1,16,256,128]{3,2,1,0:T(8,128)S(1)}, f32[1,16,256,128]{3,2,1,0:T(8,128)S(1)}, u32[]{:S(2)}, u32[]{:S(2)}) collective-permute-start(f32[1,16,256,128]{3,2,1,0:T(8,128)S(1)} %bitcast_add_fusion.2), channel_id=1, source_target_pairs={{0,252},{4,0},{8,4},{12,8},{16,12},{20,16},{24,20},{28,24},{32,28}... | collective-permute-start | bytes 6291464 | tf_op jit(solution)/shard_map/ppermute | solution.py:11
  105.2 63.2 %collective-permute-start.7 = (bf16[256,1,16,128]{3,0,2,1:T(8,128)(2,1)S(1)}, bf16[256,1,16,128]{3,0,2,1:T(8,128)(2,1)S(1)}, u32[]{:S(2)}, u32[]{:S(2)}) collective-permute-start(bf16[256,1,16,128]{3,0,2,1:T(8,128)(2,1)S(1)} %collective-permute-done.3), channel_id=1, source_target_pairs={{0,252},{4,0},{8,4},{12,8},{16,12},{20,16},{24,20},{28,24},{32,28}... | collective-permute-start | bytes 3145736 | tf_op jit(solution)/shard_map/ppermute | solution.py:11
  112.8 72.4 %collective-permute-start.12 = (f32[1,16,256]{2,1,0:T(8,128)S(1)}, f32[1,16,256]{2,1,0:T(8,128)S(1)}, u32[]{:S(2)}, u32[]{:S(2)}) collective-permute-start(f32[1,16,256]{2,1,0:T(8,128)S(1)} %bitcast_add_fusion.6), channel_id=1, source_target_pairs={{0,252},{4,0},{8,4},{12,8},{16,12},{20,16},{24,20},{28,24},{32,28}... | collective-permute-start | bytes 49160 | tf_op jit(solution)/shard_map/ppermute | solution.py:11
  113.0 62.9 %collective-permute-start.5 = (f32[1,16,256]{2,1,0:T(8,128)S(1)}, f32[1,16,256]{2,1,0:T(8,128)S(1)}, u32[]{:S(2)}, u32[]{:S(2)}) collective-permute-start(f32[1,16,256]{2,1,0:T(8,128)S(1)} %get-tuple-element.8), channel_id=1, source_target_pairs={{0,252},{4,0},{8,4},{12,8},{16,12},{20,16},{24,20},{28,24},{32,28}... | collective-permute-start | bytes 49160 | tf_op jit(solution)/shard_map/ppermute | solution.py:11
  168.4 75.7 %collective-permute-start.11 = (bf16[256,1,16,128]{3,0,2,1:T(8,128)(2,1)S(1)}, bf16[256,1,16,128]{3,0,2,1:T(8,128)(2,1)S(1)}, u32[]{:S(2)}, u32[]{:S(2)}) collective-permute-start(bf16[256,1,16,128]{3,0,2,1:T(8,128)(2,1)S(1)} %collective-permute-done.7), channel_id=1, source_target_pairs={{0,252},{4,0},{8,4},{12,8},{16,12},{20,16},{24,20},{28,24},{32,28}... | collective-permute-start | bytes 3145736 | tf_op jit(solution)/shard_map/ppermute | solution.py:11
  177.5 68.2 %collective-permute-start.8 = (f32[1,16,256,128]{3,2,1,0:T(8,128)S(1)}, f32[1,16,256,128]{3,2,1,0:T(8,128)S(1)}, u32[]{:S(2)}, u32[]{:S(2)}) collective-permute-start(f32[1,16,256,128]{3,2,1,0:T(8,128)S(1)} %bitcast_add_fusion.1), channel_id=1, source_target_pairs={{0,252},{4,0},{8,4},{12,8},{16,12},{20,16},{24,20},{28,24},{32,28}... | collective-permute-start | bytes 6291464 | tf_op jit(solution)/shard_map/ppermute | solution.py:11
  185.2 52.1 %collective-permute-start.13 = (f32[1,16,256]{2,1,0:T(8,128)S(1)}, f32[1,16,256]{2,1,0:T(8,128)S(1)}, u32[]{:S(2)}, u32[]{:S(2)}) collective-permute-start(f32[1,16,256]{2,1,0:T(8,128)S(1)} %bitcast_add_fusion.5), channel_id=1, source_target_pairs={{0,252},{4,0},{8,4},{12,8},{16,12},{20,16},{24,20},{28,24},{32,28}... | collective-permute-start | bytes 49160 | tf_op jit(solution)/shard_map/ppermute | solution.py:11
  186.1 58.7 %collective-permute-start.9 = (f32[1,16,256]{2,1,0:T(8,128)S(1)}, f32[1,16,256]{2,1,0:T(8,128)S(1)}, u32[]{:S(2)}, u32[]{:S(2)}) collective-permute-start(f32[1,16,256]{2,1,0:T(8,128)S(1)} %get-tuple-element.6), channel_id=1, source_target_pairs={{0,252},{4,0},{8,4},{12,8},{16,12},{20,16},{24,20},{28,24},{32,28}... | collective-permute-start | bytes 49160 | tf_op jit(solution)/shard_map/ppermute | solution.py:11
  237.3 8.4 %collective-permute-start.14 = (f32[1,16,256]{2,1,0:T(8,128)S(1)}, f32[1,16,256]{2,1,0:T(8,128)S(1)}, u32[]{:S(2)}, u32[]{:S(2)}) collective-permute-start(f32[1,16,256]{2,1,0:T(8,128)S(1)} %bitcast_add_fusion.4), channel_id=1, source_target_pairs={{0,252},{4,0},{8,4},{12,8},{16,12},{20,16},{24,20},{28,24},{32,28}... | collective-permute-start | bytes 49160 | tf_op jit(solution)/shard_map/ppermute | solution.py:11
  248.6 29.5 %collective-permute-start.15 = (bf16[256,2048]{0,1:T(8,128)(2,1)S(1)}, bf16[256,2048]{0,1:T(8,128)(2,1)S(1)}, u32[]{:S(2)}, u32[]{:S(2)}) collective-permute-start(bf16[256,2048]{0,1:T(8,128)(2,1)S(1)} %bitcast.195), channel_id=1, source_target_pairs={{0,12},{4,16},{8,20},{12,24},{16,28},{20,32},{24,36},{28,40},{32,4... | collective-permute-start | bytes 3145736 | tf_op jit(solution)/shard_map/ppermute | solution.py:11
where the time goes:
time: 300 us; the launch traced here: 299 us
  waiting for transfers between devices  197 us (66%)
  starting transfers between devices  63.2 us (21%)
  blocking collectives  19.6 us (7%)
  matrix products  11.4 us (4%)
  other arithmetic  5.32 us (2%)
    ppermute x16, waiting for transfers between devices, passed_along(): lax.ppermute(value, axis, [(i, (i + by) % devices) for i in range(devices)])  197 us
    ppermute x16, starting transfers between devices, passed_along(): lax.ppermute(value, axis, [(i, (i + by) % devices) for i in range(devices)])  63.2 us
    all_to_all x1, blocking collectives, body(): lax.all_to_all(finished, 'kvh', split_axis=0, concat_axis=1, tiled=True)  19.6 us
    dot_general x4, matrix products, body(): jnp.einsum('hgqk,khd->hgqd', weight.astype(jnp.bfloat16), values, preferr...  7.13 us
  transfers between devices with their start and end apart: 16, of which 7 were waited for; matrix products, arithmetic and copies ran while one was open for 3% of the time, Pallas kernels for 0%

commit v1 on v0

v1 whole, which is shorter than its diff:
```python
import functools

import jax
import jax.numpy as jnp
from jax import lax
from jax.experimental import pallas as pl
from jax.experimental.pallas import tpu as pltpu
from jax.sharding import PartitionSpec as P

MESH = pl.DeviceIdType.MESH
BACK = 3
SHARD = 256
GROUP = 16
WIDTH = 128
KEYS = (BACK + 1) * SHARD
BLOCK = 64
WINDOW = BACK * SHARD + BLOCK
TILE = 64
PIECES = BLOCK // TILE
ROWS = TILE * GROUP
HIDE = -131072.0
EXP2 = 1.4426950408889634 / WIDTH**0.5
LAST = (((1,), (1,)), ((), ()))
PLAIN = (((1,), (0,)), ((), ()))


def kernel(
    q_hbm, k_hbm, v_hbm, ids_hbm, out_hbm,
    q_buf, k_buf, v_buf, id_buf, pick, bias, stage, turned,
    load_sem, kv_send, kv_recv, out_send, out_recv, own_sem,
):
    ctx = lax.axis_index("ctx")
    kvh = lax.axis_index("kvh")
    shards = lax.axis_size("ctx")
    pair, core = kvh // 2, kvh % 2

    def behind(by):
        return (lax.rem(ctx + shards - by, shards), kvh)

    def ahead(by):
        return (lax.rem(ctx + by, shards), kvh)

    def owner(step):
        late, odd = step // 2, step % 2
        x = (1 - pair) * (1 - late) + pair * late
        c = (1 - odd) * (1 - late) + late * ((1 - core) * (1 - odd) + core * odd)
        return 2 * x + c

    barrier = pltpu.get_barrier_semaphore()
    for by in range(1, BACK + 1):
        pl.semaphore_signal(barrier, inc=1, device_id=behind(by), device_id_type=MESH)
    for step in range(3):
        pl.semaphore_signal(barrier, inc=1, device_id=(ctx, owner(step)), device_id_type=MESH)

    own = BACK * SHARD
    loads = [
        pltpu.make_async_copy(ids_hbm, id_buf.at[BACK], load_sem.at[0]),
        pltpu.make_async_copy(k_hbm, k_buf.at[pl.ds(own, SHARD)], load_sem.at[1]),
        pltpu.make_async_copy(v_hbm, v_buf.at[pl.ds(own, SHARD)], load_sem.at[2]),
        pltpu.make_async_copy(q_hbm, q_buf, load_sem.at[3]),
    ]
    for load in loads:
        load.start()

    pl.semaphore_wait(barrier, BACK + 3)
    moves = []
    for by in range(1, BACK + 1):
        to = BACK - by
        rows = pl.ds(to * SHARD, SHARD)
        for i, (src, dst) in enumerate(
            [(ids_hbm, id_buf.at[to]), (k_hbm, k_buf.at[rows]), (v_hbm, v_buf.at[rows])]
        ):
            moves.append(
                pltpu.make_async_remote_copy(
                    src_ref=src, dst_ref=dst, send_sem=kv_send.at[to, i], recv_sem=kv_recv.at[to, i],
                    device_id=ahead(by), device_id_type=MESH,
                )
            )
    for move in moves:
        move.start()

    token = lax.broadcasted_iota(jnp.int32, (SHARD // 2 * GROUP, WIDTH), 0) // GROUP
    lane = lax.broadcasted_iota(jnp.int32, (SHARD // 2 * GROUP, WIDTH), 1)
    pick[...] = jnp.where(token == lane, 1.0, 0.0).astype(jnp.bfloat16)

    def hide(part):
        for r in range(2):
            row = id_buf[part, r : r + 1, :].astype(jnp.float32)
            column = jnp.broadcast_to(row, (WIDTH, WIDTH)).T
            at = part * SHARD + r * WIDTH
            key_pos = lax.broadcasted_iota(jnp.int32, (WIDTH, WIDTH), 0) + at
            query_pos = lax.broadcasted_iota(jnp.int32, (WIDTH, WIDTH), 1) + own
            for half in range(2):
                query = id_buf[BACK, half : half + 1, :].astype(jnp.float32)
                seen = column == query
                if part == BACK:
                    seen = seen & (key_pos <= query_pos + half * WIDTH)
                bias[half, pl.ds(at, WIDTH), :] = jnp.where(seen, 0.0, HIDE).astype(jnp.bfloat16)

    loads[0].wait()
    hide(BACK)
    for i in range(0, len(moves), 3):
        moves[i].wait_recv()
    for part in range(BACK):
        hide(part)
    for load in loads[1:]:
        load.wait()
    for i in range(0, len(moves), 3):
        moves[i + 1].wait_recv()
        moves[i + 2].wait_recv()

    def outgoing(step, piece):
        rows = pl.ds(pl.multiple_of(piece * TILE, TILE), TILE)
        slot = core * (1 - step // 2) + 2 * (step // 2)
        return pltpu.make_async_remote_copy(
            src_ref=stage.at[step, rows],
            dst_ref=out_hbm.at[rows, pl.ds(pl.multiple_of(kvh * GROUP * WIDTH, WIDTH), GROUP * WIDTH)],
            send_sem=out_send.at[step, piece], recv_sem=out_recv.at[slot, piece],
            device_id=(ctx, owner(step)), device_id_type=MESH,
        )

    def kept(piece):
        rows = pl.ds(pl.multiple_of(piece * TILE, TILE), TILE)
        return pltpu.make_async_copy(
            stage.at[3, rows],
            out_hbm.at[rows, pl.ds(pl.multiple_of(kvh * GROUP * WIDTH, WIDTH), GROUP * WIDTH)],
            own_sem.at[piece],
        )

    def work(i, _):
        step, piece = i // PIECES, i % PIECES
        block = owner(step)
        window = pl.ds(pl.multiple_of(block * BLOCK, BLOCK), WINDOW)
        keys = jnp.concatenate([k_buf[window, :], bias[block // 2, window, :]], axis=1)
        ones = jnp.ones((16, WINDOW), jnp.bfloat16)
        values = jnp.concatenate([v_buf[window, :].T, ones], axis=0)
        first = pl.multiple_of((block * PIECES + piece) * ROWS, ROWS)
        inside = pl.multiple_of(((block % 2) * PIECES + piece) * ROWS, ROWS)
        queries = jnp.concatenate([q_buf[pl.ds(first, ROWS), :], pick[pl.ds(inside, ROWS), :]], axis=1)
        score = lax.dot_general(keys, queries, LAST, preferred_element_type=jnp.float32)
        top = jnp.max(score, axis=0, keepdims=True)
        weight = jnp.exp2((score - top) * EXP2).astype(jnp.bfloat16)
        summed = lax.dot_general(values, weight, PLAIN, preferred_element_type=jnp.float32)
        turned[...] = (summed[:WIDTH] / summed[WIDTH : WIDTH + 1]).T
        tokens = pl.ds(pl.multiple_of(piece * TILE, TILE), TILE)
        for head in range(GROUP):
            stage[step, tokens, head * WIDTH : (head + 1) * WIDTH] = turned[
                pl.ds(head, TILE, stride=GROUP), :
            ].astype(jnp.bfloat16)

        @pl.when(step < 3)
        def _():
            outgoing(step, piece).start()

        @pl.when(step == 3)
        def _():
            kept(piece).start()

        return 0

    lax.fori_loop(0, 4 * PIECES, work, 0)

    for move in moves:
        move.wait_send()
    for piece in range(PIECES):
        kept(piece).wait()
        for step in range(3):
            outgoing(step, piece).wait_send()
        for slot in range(3):
            rows = pl.ds(piece * TILE, TILE)
            pltpu.make_async_remote_copy(
                src_ref=stage.at[slot, rows], dst_ref=out_hbm.at[rows, pl.ds(0, GROUP * WIDTH)],
                send_sem=out_send.at[slot, piece], recv_sem=out_recv.at[slot, piece],
                device_id=(ctx, owner(0)), device_id_type=MESH,
            ).wait_recv()


def body(queries, keys, values, doc_ids):
    anywhere = pl.BlockSpec(memory_space=pl.ANY)
    return pl.pallas_call(
        kernel,
        name="attend",
        out_shape=jax.ShapeDtypeStruct((BLOCK, 4 * GROUP * WIDTH), jnp.bfloat16),
        in_specs=[anywhere] * 4,
        out_specs=anywhere,
        scratch_shapes=[
            pltpu.VMEM((SHARD * GROUP, WIDTH), jnp.bfloat16),
            pltpu.VMEM((KEYS, WIDTH), jnp.bfloat16),
            pltpu.VMEM((KEYS, WIDTH), jnp.bfloat16),
            pltpu.VMEM((BACK + 1, 2, WIDTH), jnp.int32),
            pltpu.VMEM((SHARD // 2 * GROUP, WIDTH), jnp.bfloat16),
            pltpu.VMEM((2, KEYS, WIDTH), jnp.bfloat16),
            pltpu.VMEM((4, BLOCK, GROUP * WIDTH), jnp.bfloat16),
            pltpu.VMEM((ROWS, WIDTH), jnp.float32),
            pltpu.SemaphoreType.DMA((4,)),
            pltpu.SemaphoreType.DMA((BACK, 3)),
            pltpu.SemaphoreType.DMA((BACK, 3)),
            pltpu.SemaphoreType.DMA((3, PIECES)),
            pltpu.SemaphoreType.DMA((3, PIECES)),
            pltpu.SemaphoreType.DMA((PIECES,)),
        ],
        compiler_params=pltpu.CompilerParams(
            collective_id=0, has_side_effects=True, vmem_limit_bytes=56 << 20
        ),
        cost_estimate=pl.CostEstimate(
            flops=4 * SHARD * GROUP * KEYS * WIDTH, bytes_accessed=4 << 20, transcendentals=SHARD * GROUP * KEYS
        ),
    )(
        queries.reshape(SHARD * GROUP, WIDTH),
        keys.reshape(SHARD, WIDTH),
        values.reshape(SHARD, WIDTH),
        doc_ids.reshape(2, WIDTH),
    )


def solution(mesh):
    return jax.shard_map(
        body,
        mesh=mesh,
        in_specs=(P("ctx", "kvh", None), P("ctx", "kvh", None), P("ctx", "kvh", None), P("ctx")),
        out_specs=P(("ctx", "kvh"), None),
        check_vma=False,
    )
```

time: 300 us -> 39.2 us (0.13)
  the two profiles are of different devices: /device:TPU:8 before, /device:TPU:16 now
where the time goes in v1:
time: 39.2 us; the launch traced here: 39.1 us
  Pallas kernels  36.8 us (94%)
  local copies, waits for them, and re-layouts  2.26 us (6%)
    pallas_call x1, Pallas kernels, body(): pl.pallas_call(kernel, name='attend', out_shape=jax.ShapeDtypeStruct((BLO...  36.8 us
    unnamed x1, local copies, waits for them, and re-layouts  2.26 us

profile of v1, /device:TPU:16, one launch (start us, length us, event | category | flops | bytes accessed | tf_op | source)
XLA Modules:
  0.0 39.1 jit_solution(13765473117996057396)
XLA Ops:
  0.0 36.8 %attend.1 = bf16[64,8192]{1,0:T(8,128)(2,1)} custom-call(bf16[4096,128]{1,0:T(8,128)(2,1)} %bitcast.4, bf16[256,128]{1,0:T(8,128)(2,1)} %bitcast.5, bf16[256,128]{1,0:T(8,128)(2,1)} %bitcast.6, s32[2,128]{1,0:T(2,128)} %bitcast.7), custom_call_target="tpu_custom_call" | custom-call | flops 2147483648 | bytes 4194304 | tf_op jit(solution)/shard_map/attend/pallas_call | solution.py:180
  36.8 2.3 %copy.6 = bf16[64,8192]{1,0:T(8,128)(2,1)} copy(bf16[64,8192]{1,0:T(8,128)(2,1)} %attend.1) | data formatting | bytes 2097152

commit v2 on v1

--- a/solution.py
+++ b/solution.py
@@ -9,13 +9,17 @@
 
 MESH = pl.DeviceIdType.MESH
 BACK = 3
+RING = 4
+CROSS = [(y, by) for y in range(RING) for by in range(1, BACK + 1) if y + by >= RING]
+DIRECT = [(1,3),(2,2),(2,3),(3,1)]
+PASSED = [flow for flow in CROSS if flow not in DIRECT]
 SHARD = 256
 GROUP = 16
 WIDTH = 128
 KEYS = (BACK + 1) * SHARD
 BLOCK = 64
 WINDOW = BACK * SHARD + BLOCK
-TILE = 64
+TILE = 32
 PIECES = BLOCK // TILE
 ROWS = TILE * GROUP
 HIDE = -131072.0
@@ -26,7 +30,7 @@
 
 def kernel(
     q_hbm, k_hbm, v_hbm, ids_hbm, out_hbm,
-    q_buf, k_buf, v_buf, id_buf, pick, bias, stage, turned,
+    q_buf, k_buf, v_buf, id_buf, k_pass, v_pass, id_pass, pick, bias, stage, turned,
     load_sem, kv_send, kv_recv, out_send, out_recv, own_sem,
 ):
     ctx = lax.axis_index("ctx")
@@ -34,11 +38,18 @@
     shards = lax.axis_size("ctx")
     pair, core = kvh // 2, kvh % 2
 
-    def behind(by):
-        return (lax.rem(ctx + shards - by, shards), kvh)
-
-    def ahead(by):
-        return (lax.rem(ctx + by, shards), kvh)
+    ring, place = ctx // RING, ctx % RING
+    rings = shards // RING
+
+    def any_of(conditions):
+        return functools.reduce(jnp.logical_or, conditions, False)
+
+    takes = (ring >= 1) & any_of([place == y for y in sorted({y for y, _ in PASSED})])
+    gives = (ring < rings - 1) & any_of([place == y for y in sorted({y for y, _ in PASSED})])
+    straight = {by: (place + by < RING) | ((ring < rings - 1) & any_of([place == y for y, b in DIRECT if b == by])) for by in range(1, BACK + 1)}
+    reached = {by: (place >= by) | ((ring >= 1) & any_of([place == y + by - RING for y, b in DIRECT if b == by])) for by in range(1, BACK + 1)}
+    onward = {by: takes & any_of([place == y for y, b in PASSED if b == by]) for by in range(1, BACK + 1)}
+    fed = {by: (ring >= 1) & any_of([place == y + by - RING for y, b in PASSED if b == by]) for by in range(1, BACK + 1)}
 
     def owner(step):
         late, odd = step // 2, step % 2
@@ -48,9 +59,21 @@
 
     barrier = pltpu.get_barrier_semaphore()
     for by in range(1, BACK + 1):
-        pl.semaphore_signal(barrier, inc=1, device_id=behind(by), device_id_type=MESH)
+
+        @pl.when(reached[by])
+        def _():
+            pl.semaphore_signal(barrier, inc=1, device_id=(ctx - by, kvh), device_id_type=MESH)
+
+        @pl.when(fed[by])
+        def _():
+            pl.semaphore_signal(barrier, inc=1, device_id=(ctx - by + RING, kvh), device_id_type=MESH)
+
     for step in range(3):
         pl.semaphore_signal(barrier, inc=1, device_id=(ctx, owner(step)), device_id_type=MESH)
+
+    @pl.when(takes)
+    def _():
+        pl.semaphore_signal(barrier, inc=1, device_id=(ctx - RING, kvh), device_id_type=MESH)
 
     own = BACK * SHARD
     loads = [
@@ -62,52 +85,89 @@
     for load in loads:
         load.start()
 
-    pl.semaphore_wait(barrier, BACK + 3)
-    moves = []
-    for by in range(1, BACK + 1):
-        to = BACK - by
+    sent_to = [gives, *straight.values(), *onward.values()]
+    pl.semaphore_wait(barrier, 3 + sum(to.astype(jnp.int32) for to in sent_to))
+
+    def part(i, to):
+        if to == BACK + 1:
+            return (id_pass, k_pass, v_pass)[i]
         rows = pl.ds(to * SHARD, SHARD)
-        for i, (src, dst) in enumerate(
-            [(ids_hbm, id_buf.at[to]), (k_hbm, k_buf.at[rows]), (v_hbm, v_buf.at[rows])]
-        ):
-            moves.append(
-                pltpu.make_async_remote_copy(
-                    src_ref=src, dst_ref=dst, send_sem=kv_send.at[to, i], recv_sem=kv_recv.at[to, i],
-                    device_id=ahead(by), device_id_type=MESH,
-                )
-            )
-    for move in moves:
-        move.start()
+        return (id_buf.at[to], k_buf.at[rows], v_buf.at[rows])[i]
+
+    def move(i, to, target, passed):
+        src = part(i, BACK + 1) if passed else (ids_hbm, k_hbm, v_hbm)[i]
+        return pltpu.make_async_remote_copy(
+            src_ref=src, dst_ref=part(i, to),
+            send_sem=kv_send.at[(to if to <= BACK - 1 else BACK) + (BACK + 1) * passed, i], recv_sem=kv_recv.at[to if to <= BACK - 1 else BACK, i],
+            device_id=(target, kvh), device_id_type=MESH,
+        )
+
+    @pl.when(gives)
+    def _():
+        for i in range(3):
+            move(i, BACK + 1, ctx + RING, False).start()
+
+    for by in range(1, BACK + 1):
+
+        @pl.when(straight[by])
+        def _():
+            for i in range(3):
+                move(i, BACK - by, ctx + by, False).start()
+
+    for by in range(1, BACK + 1):
+
+        @pl.when(ctx < by)
+        def _():
+            rows = pl.ds((BACK - by) * SHARD, SHARD)
+            id_buf[BACK - by] = jnp.full((2, WIDTH), -1, jnp.int32)
+            k_buf[rows] = jnp.zeros((SHARD, WIDTH), jnp.bfloat16)
+            v_buf[rows] = jnp.zeros((SHARD, WIDTH), jnp.bfloat16)
+
+    @pl.when(takes)
+    def _():
+        for i in range(3):
+            move(i, BACK + 1, ctx, False).wait_recv()
+            for by in range(1, BACK + 1):
+
+                @pl.when(onward[by])
+                def _():
+                    move(i, BACK - by, ctx + by - RING, True).start()
 
     token = lax.broadcasted_iota(jnp.int32, (SHARD // 2 * GROUP, WIDTH), 0) // GROUP
     lane = lax.broadcasted_iota(jnp.int32, (SHARD // 2 * GROUP, WIDTH), 1)
     pick[...] = jnp.where(token == lane, 1.0, 0.0).astype(jnp.bfloat16)
 
-    def hide(part):
+    def hide(part_of):
         for r in range(2):
-            row = id_buf[part, r : r + 1, :].astype(jnp.float32)
+            row = id_buf[part_of, r : r + 1, :].astype(jnp.float32)
             column = jnp.broadcast_to(row, (WIDTH, WIDTH)).T
-            at = part * SHARD + r * WIDTH
+            at = part_of * SHARD + r * WIDTH
             key_pos = lax.broadcasted_iota(jnp.int32, (WIDTH, WIDTH), 0) + at
             query_pos = lax.broadcasted_iota(jnp.int32, (WIDTH, WIDTH), 1) + own
             for half in range(2):
                 query = id_buf[BACK, half : half + 1, :].astype(jnp.float32)
                 seen = column == query
-                if part == BACK:
+                if part_of == BACK:
                     seen = seen & (key_pos <= query_pos + half * WIDTH)
                 bias[half, pl.ds(at, WIDTH), :] = jnp.where(seen, 0.0, HIDE).astype(jnp.bfloat16)
 
     loads[0].wait()
     hide(BACK)
-    for i in range(0, len(moves), 3):
-        moves[i].wait_recv()
-    for part in range(BACK):
-        hide(part)
+    for by in range(1, BACK + 1):
+
+        @pl.when(ctx >= by)
+        def _():
+            move(0, BACK - by, ctx, False).wait_recv()
+
+        hide(BACK - by)
     for load in loads[1:]:
         load.wait()
-    for i in range(0, len(moves), 3):
-        moves[i + 1].wait_recv()
-        moves[i + 2].wait_recv()
+    for by in range(1, BACK + 1):
+
+        @pl.when(ctx >= by)
+        def _():
+            move(1, BACK - by, ctx, False).wait_recv()
+            move(2, BACK - by, ctx, False).wait_recv()
 
     def outgoing(step, piece):
         rows = pl.ds(pl.multiple_of(piece * TILE, TILE), TILE)
@@ -160,8 +220,21 @@
 
     lax.fori_loop(0, 4 * PIECES, work, 0)
 
-    for move in moves:
-        move.wait_send()
+    for i in range(3):
+        for by in range(1, BACK + 1):
+
+            @pl.when(straight[by])
+            def _():
+                move(i, BACK - by, ctx, False).wait_send()
+
+            @pl.when(onward[by])
+            def _():
+                move(i, BACK - by, ctx, True).wait_send()
+
+        @pl.when(gives)
+        def _():
+            move(i, BACK + 1, ctx, False).wait_send()
+
     for piece in range(PIECES):
         kept(piece).wait()
         for step in range(3):
@@ -180,21 +253,24 @@
     return pl.pallas_call(
         kernel,
         name="attend",
-        out_shape=jax.ShapeDtypeStruct((BLOCK, 4 * GROUP * WIDTH), jnp.bfloat16),
+        out_shape=pltpu.VMEM((BLOCK, 4 * GROUP * WIDTH), jnp.bfloat16),
         in_specs=[anywhere] * 4,
-        out_specs=anywhere,
+        out_specs=pl.BlockSpec(memory_space=pltpu.VMEM),
         scratch_shapes=[
             pltpu.VMEM((SHARD * GROUP, WIDTH), jnp.bfloat16),
             pltpu.VMEM((KEYS, WIDTH), jnp.bfloat16),
             pltpu.VMEM((KEYS, WIDTH), jnp.bfloat16),
             pltpu.VMEM((BACK + 1, 2, WIDTH), jnp.int32),
+            pltpu.VMEM((SHARD, WIDTH), jnp.bfloat16),
+            pltpu.VMEM((SHARD, WIDTH), jnp.bfloat16),
+            pltpu.VMEM((2, WIDTH), jnp.int32),
             pltpu.VMEM((SHARD // 2 * GROUP, WIDTH), jnp.bfloat16),
             pltpu.VMEM((2, KEYS, WIDTH), jnp.bfloat16),
             pltpu.VMEM((4, BLOCK, GROUP * WIDTH), jnp.bfloat16),
             pltpu.VMEM((ROWS, WIDTH), jnp.float32),
             pltpu.SemaphoreType.DMA((4,)),
-            pltpu.SemaphoreType.DMA((BACK, 3)),
-            pltpu.SemaphoreType.DMA((BACK, 3)),
+            pltpu.SemaphoreType.DMA((2 * BACK + 1, 3)),
+            pltpu.SemaphoreType.DMA((BACK + 1, 3)),
             pltpu.SemaphoreType.DMA((3, PIECES)),
             pltpu.SemaphoreType.DMA((3, PIECES)),
             pltpu.SemaphoreType.DMA((PIECES,)),

time: 39.2 us -> 30.1 us (0.77)
  the two profiles are of different devices: /device:TPU:16 before, /device:TPU:224 now
where the time goes in v2:
time: 30.1 us; the launch traced here: 29.6 us
  Pallas kernels  28.7 us (95%)
  local copies, waits for them, and re-layouts  0.97 us (3%)
    pallas_call x1, Pallas kernels, body(): pl.pallas_call(kernel, name='attend', out_shape=pltpu.VMEM((BLOCK, 4 * GR...  28.7 us
    unnamed x1, local copies, waits for them, and re-layouts  0.97 us

profile of v2, /device:TPU:224, one launch (start us, length us, event | category | flops | bytes accessed | tf_op | source)
XLA Modules:
  0.0 29.6 jit_solution(13305736700160792178)
XLA Ops:
  0.0 28.7 %attend.1 = bf16[64,8192]{1,0:T(8,128)(2,1)S(1)} custom-call(bf16[4096,128]{1,0:T(8,128)(2,1)} %bitcast.4, bf16[256,128]{1,0:T(8,128)(2,1)} %bitcast.5, bf16[256,128]{1,0:T(8,128)(2,1)} %bitcast.6, s32[2,128]{1,0:T(2,128)} %bitcast.7), custom_call_target="tpu_custom_call" | custom-call | flops 2147483648 | bytes 4194304 | tf_op jit(solution)/shard_map/attend/pallas_call | solution.py:253
  28.7 1.0 %copy.6 = bf16[64,8192]{1,0:T(8,128)(2,1)} copy(bf16[64,8192]{1,0:T(8,128)(2,1)S(1)} %attend.1) | data formatting | bytes 2097152

commit v3 on v2

--- a/solution.py
+++ b/solution.py
@@ -11,14 +11,17 @@
 BACK = 3
 RING = 4
 CROSS = [(y, by) for y in range(RING) for by in range(1, BACK + 1) if y + by >= RING]
-DIRECT = [(1,3),(2,2),(2,3),(3,1)]
-PASSED = [flow for flow in CROSS if flow not in DIRECT]
+DIRECT = ([(1, 3), (2, 2), (2, 3), (3, 1)], [(1, 3), (2, 2), (2, 3), (3, 1)])
+PASSED = [[flow for flow in CROSS if flow not in straight] for straight in DIRECT]
 SHARD = 256
+CUTS = 1
+CUT = SHARD // CUTS
+ITEMS = 1 + 2 * CUTS
 GROUP = 16
 WIDTH = 128
 KEYS = (BACK + 1) * SHARD
 BLOCK = 64
-WINDOW = BACK * SHARD + BLOCK
+WINDOW = BACK * SHARD + 2 * BLOCK
 TILE = 32
 PIECES = BLOCK // TILE
 ROWS = TILE * GROUP
@@ -30,7 +33,7 @@
 
 def kernel(
     q_hbm, k_hbm, v_hbm, ids_hbm, out_hbm,
-    q_buf, k_buf, v_buf, id_buf, k_pass, v_pass, id_pass, pick, bias, stage, turned,
+    q_buf, k_buf, v_buf, id_buf, vt_buf, k_pass, v_pass, id_pass, pick, bias, stage, turned,
     load_sem, kv_send, kv_recv, out_send, out_recv, own_sem,
 ):
     ctx = lax.axis_index("ctx")
@@ -44,12 +47,24 @@
     def any_of(conditions):
         return functools.reduce(jnp.logical_or, conditions, False)
 
-    takes = (ring >= 1) & any_of([place == y for y in sorted({y for y, _ in PASSED})])
-    gives = (ring < rings - 1) & any_of([place == y for y in sorted({y for y, _ in PASSED})])
-    straight = {by: (place + by < RING) | ((ring < rings - 1) & any_of([place == y for y, b in DIRECT if b == by])) for by in range(1, BACK + 1)}
-    reached = {by: (place >= by) | ((ring >= 1) & any_of([place == y + by - RING for y, b in DIRECT if b == by])) for by in range(1, BACK + 1)}
-    onward = {by: takes & any_of([place == y for y, b in PASSED if b == by]) for by in range(1, BACK + 1)}
-    fed = {by: (ring >= 1) & any_of([place == y + by - RING for y, b in PASSED if b == by]) for by in range(1, BACK + 1)}
+    def sends(flows, by=None):
+        found = [(ring % 2 == i) & (place == y) for i in range(2) for y in sorted({y for y, b in flows[i] if by in (None, b)})]
+        return (ring < rings - 1) & any_of(found)
+
+    def after(flows, by=None, end=False):
+        found = [
+            (ring % 2 == 1 - i) & (place == y)
+            for i in range(2)
+            for y in sorted({y + (b - RING) * end for y, b in flows[i] if by in (None, b)})
+        ]
+        return (ring >= 1) & any_of(found)
+
+    steps = range(1, BACK + 1)
+    gives, takes = sends(PASSED), after(PASSED)
+    straight = {by: (place + by < RING) | sends(DIRECT, by) for by in steps}
+    reached = {by: (place >= by) | after(DIRECT, by, end=True) for by in steps}
+    onward = {by: after(PASSED, by) for by in steps}
+    fed = {by: after(PASSED, by, end=True) for by in steps}
 
     def owner(step):
         late, odd = step // 2, step % 2
@@ -88,30 +103,42 @@
     sent_to = [gives, *straight.values(), *onward.values()]
     pl.semaphore_wait(barrier, 3 + sum(to.astype(jnp.int32) for to in sent_to))
 
+    def part_rows(to, first=0, count=SHARD):
+        return pl.ds(pl.multiple_of(to * SHARD + first, WIDTH), count)
+
     def part(i, to):
-        if to == BACK + 1:
-            return (id_pass, k_pass, v_pass)[i]
-        rows = pl.ds(to * SHARD, SHARD)
-        return (id_buf.at[to], k_buf.at[rows], v_buf.at[rows])[i]
+        if isinstance(to, int) and to == BACK + 1:
+            return id_pass if i == 0 else (k_pass, v_pass)[(i - 1) // CUTS].at[pl.ds((i - 1) % CUTS * CUT, CUT)]
+        if i == 0:
+            return id_buf.at[to]
+        return (k_buf, v_buf)[(i - 1) // CUTS].at[part_rows(to, (i - 1) % CUTS * CUT, CUT)]
 
     def move(i, to, target, passed):
-        src = part(i, BACK + 1) if passed else (ids_hbm, k_hbm, v_hbm)[i]
+        src = ids_hbm if i == 0 else (k_hbm, v_hbm)[(i - 1) // CUTS].at[pl.ds((i - 1) % CUTS * CUT, CUT)]
+        slot = BACK if isinstance(to, int) and to > BACK else to
+        if passed:
+            src = part(i, BACK + 1)
         return pltpu.make_async_remote_copy(
             src_ref=src, dst_ref=part(i, to),
-            send_sem=kv_send.at[(to if to <= BACK - 1 else BACK) + (BACK + 1) * passed, i], recv_sem=kv_recv.at[to if to <= BACK - 1 else BACK, i],
+            send_sem=kv_send.at[slot + (BACK + 1) * passed, i], recv_sem=kv_recv.at[slot, i],
             device_id=(target, kvh), device_id_type=MESH,
         )
 
     @pl.when(gives)
     def _():
-        for i in range(3):
+        for i in range(ITEMS):
             move(i, BACK + 1, ctx + RING, False).start()
 
-    for by in range(1, BACK + 1):
-
-        @pl.when(straight[by])
-        def _():
-            for i in range(3):
+    @pl.when(straight[1])
+    def _():
+        for i in range(ITEMS):
+            move(i, BACK - 1, ctx + 1, False).start()
+
+    for i in range(ITEMS):
+        for by in (2, 3):
+
+            @pl.when(straight[by])
+            def _():
                 move(i, BACK - by, ctx + by, False).start()
 
     for by in range(1, BACK + 1):
@@ -123,51 +150,48 @@
             k_buf[rows] = jnp.zeros((SHARD, WIDTH), jnp.bfloat16)
             v_buf[rows] = jnp.zeros((SHARD, WIDTH), jnp.bfloat16)
 
+    token = lax.broadcasted_iota(jnp.int32, (SHARD // 2 * GROUP, WIDTH), 0) // GROUP
+    lane = lax.broadcasted_iota(jnp.int32, (SHARD // 2 * GROUP, WIDTH), 1)
+    pick[...] = jnp.where(token == lane, 1.0, 0.0).astype(jnp.bfloat16)
+
+    def hide(to, causal=False):
+        for r in range(2):
+            row = id_buf[to, r : r + 1, :].astype(jnp.float32)
+            column = jnp.broadcast_to(row, (WIDTH, WIDTH)).T
+            key_pos = lax.broadcasted_iota(jnp.int32, (WIDTH, WIDTH), 0) + r * WIDTH
+            query_pos = lax.broadcasted_iota(jnp.int32, (WIDTH, WIDTH), 1)
+            for half in range(2):
+                query = id_buf[BACK, half : half + 1, :].astype(jnp.float32)
+                seen = column == query
+                if causal:
+                    seen = seen & (key_pos <= query_pos + half * WIDTH)
+                rows = part_rows(to, r * WIDTH, WIDTH)
+                bias[half, rows, :] = jnp.where(seen, 0.0, HIDE).astype(jnp.bfloat16)
+
+    def turn(to):
+        vt_buf[:WIDTH, part_rows(to)] = v_buf[part_rows(to), :].T
+
+    def arrived(to, items):
+        @pl.when(ctx >= BACK - to)
+        def _():
+            for i in items:
+                move(i, to, ctx, False).wait_recv()
+
+    vt_buf[WIDTH:, :] = jnp.ones((16, KEYS), jnp.bfloat16)
+    for load in loads:
+        load.wait()
+    hide(BACK, causal=True)
+    turn(BACK)
+
     @pl.when(takes)
     def _():
-        for i in range(3):
+        for i in range(ITEMS):
             move(i, BACK + 1, ctx, False).wait_recv()
             for by in range(1, BACK + 1):
 
                 @pl.when(onward[by])
                 def _():
                     move(i, BACK - by, ctx + by - RING, True).start()
-
-    token = lax.broadcasted_iota(jnp.int32, (SHARD // 2 * GROUP, WIDTH), 0) // GROUP
-    lane = lax.broadcasted_iota(jnp.int32, (SHARD // 2 * GROUP, WIDTH), 1)
-    pick[...] = jnp.where(token == lane, 1.0, 0.0).astype(jnp.bfloat16)
-
-    def hide(part_of):
-        for r in range(2):
-            row = id_buf[part_of, r : r + 1, :].astype(jnp.float32)
-            column = jnp.broadcast_to(row, (WIDTH, WIDTH)).T
-            at = part_of * SHARD + r * WIDTH
-            key_pos = lax.broadcasted_iota(jnp.int32, (WIDTH, WIDTH), 0) + at
-            query_pos = lax.broadcasted_iota(jnp.int32, (WIDTH, WIDTH), 1) + own
-            for half in range(2):
-                query = id_buf[BACK, half : half + 1, :].astype(jnp.float32)
-                seen = column == query
-                if part_of == BACK:
-                    seen = seen & (key_pos <= query_pos + half * WIDTH)
-                bias[half, pl.ds(at, WIDTH), :] = jnp.where(seen, 0.0, HIDE).astype(jnp.bfloat16)
-
-    loads[0].wait()
-    hide(BACK)
-    for by in range(1, BACK + 1):
-
-        @pl.when(ctx >= by)
-        def _():
-            move(0, BACK - by, ctx, False).wait_recv()
-
-        hide(BACK - by)
-    for load in loads[1:]:
-        load.wait()
-    for by in range(1, BACK + 1):
-
-        @pl.when(ctx >= by)
-        def _():
-            move(1, BACK - by, ctx, False).wait_recv()
-            move(2, BACK - by, ctx, False).wait_recv()
 
     def outgoing(step, piece):
         rows = pl.ds(pl.multiple_of(piece * TILE, TILE), TILE)
@@ -187,20 +211,20 @@
             own_sem.at[piece],
         )
 
-    def work(i, _):
-        step, piece = i // PIECES, i % PIECES
+    def asked(step, piece):
         block = owner(step)
-        window = pl.ds(pl.multiple_of(block * BLOCK, BLOCK), WINDOW)
-        keys = jnp.concatenate([k_buf[window, :], bias[block // 2, window, :]], axis=1)
-        ones = jnp.ones((16, WINDOW), jnp.bfloat16)
-        values = jnp.concatenate([v_buf[window, :].T, ones], axis=0)
         first = pl.multiple_of((block * PIECES + piece) * ROWS, ROWS)
         inside = pl.multiple_of(((block % 2) * PIECES + piece) * ROWS, ROWS)
-        queries = jnp.concatenate([q_buf[pl.ds(first, ROWS), :], pick[pl.ds(inside, ROWS), :]], axis=1)
-        score = lax.dot_general(keys, queries, LAST, preferred_element_type=jnp.float32)
-        top = jnp.max(score, axis=0, keepdims=True)
+        return jnp.concatenate([q_buf[pl.ds(first, ROWS), :], pick[pl.ds(inside, ROWS), :]], axis=1)
+
+    def scores(keys, queries):
+        return lax.dot_general(keys, queries, LAST, preferred_element_type=jnp.float32)
+
+    def weighed(values, score, top):
         weight = jnp.exp2((score - top) * EXP2).astype(jnp.bfloat16)
-        summed = lax.dot_general(values, weight, PLAIN, preferred_element_type=jnp.float32)
+        return lax.dot_general(values, weight, PLAIN, preferred_element_type=jnp.float32)
+
+    def finish(step, piece, summed):
         turned[...] = (summed[:WIDTH] / summed[WIDTH : WIDTH + 1]).T
         tokens = pl.ds(pl.multiple_of(piece * TILE, TILE), TILE)
         for head in range(GROUP):
@@ -208,6 +232,39 @@
                 pl.ds(head, TILE, stride=GROUP), :
             ].astype(jnp.bfloat16)
 
+    late = (BACK - 1 - place) * (1 - place // BACK)
+    early = [1 - (late + 1) // 2, 2 - late // 2, BACK]
+    for to in early[:2]:
+        arrived(to, range(ITEMS))
+        hide(to)
+        turn(to)
+    half = owner(0) // 2
+    queries = asked(0, 0)
+
+    def keys_of(to):
+        return jnp.concatenate([k_buf[part_rows(to), :], bias[half, part_rows(to), :]], axis=1)
+
+    score = scores(jnp.concatenate([keys_of(to) for to in early], axis=0), queries)
+    early_top = jnp.max(score, axis=0, keepdims=True)
+    early_sum = weighed(jnp.concatenate([vt_buf[:, part_rows(to)] for to in early], axis=1), score, early_top)
+    arrived(late, [0])
+    hide(late)
+    arrived(late, range(1, ITEMS))
+    turn(late)
+    score = scores(keys_of(late), queries)
+    top = jnp.maximum(early_top, jnp.max(score, axis=0, keepdims=True))
+    late_sum = weighed(vt_buf[:, part_rows(late)], score, top)
+    finish(0, 0, early_sum * jnp.exp2((early_top - top) * EXP2) + late_sum)
+    outgoing(0, 0).start()
+
+    def work(i, _):
+        step, piece = i // PIECES, i % PIECES
+        block = owner(step)
+        window = pl.ds(pl.multiple_of(block // 2 * WIDTH, WIDTH), WINDOW)
+        score = scores(jnp.concatenate([k_buf[window, :], bias[block // 2, window, :]], axis=1), asked(step, piece))
+        top = jnp.max(score, axis=0, keepdims=True)
+        finish(step, piece, weighed(vt_buf[:, window], score, top))
+
         @pl.when(step < 3)
         def _():
             outgoing(step, piece).start()
@@ -218,9 +275,9 @@
 
         return 0
 
-    lax.fori_loop(0, 4 * PIECES, work, 0)
-
-    for i in range(3):
+    lax.fori_loop(1, 4 * PIECES, work, 0)
+
+    for i in range(ITEMS):
         for by in range(1, BACK + 1):
 
             @pl.when(straight[by])
@@ -261,6 +318,7 @@
             pltpu.VMEM((KEYS, WIDTH), jnp.bfloat16),
             pltpu.VMEM((KEYS, WIDTH), jnp.bfloat16),
             pltpu.VMEM((BACK + 1, 2, WIDTH), jnp.int32),
+            pltpu.VMEM((WIDTH + 16, KEYS), jnp.bfloat16),
             pltpu.VMEM((SHARD, WIDTH), jnp.bfloat16),
             pltpu.VMEM((SHARD, WIDTH), jnp.bfloat16),
             pltpu.VMEM((2, WIDTH), jnp.int32),
@@ -269,8 +327,8 @@
             pltpu.VMEM((4, BLOCK, GROUP * WIDTH), jnp.bfloat16),
             pltpu.VMEM((ROWS, WIDTH), jnp.float32),
             pltpu.SemaphoreType.DMA((4,)),
-            pltpu.SemaphoreType.DMA((2 * BACK + 1, 3)),
-            pltpu.SemaphoreType.DMA((BACK + 1, 3)),
+            pltpu.SemaphoreType.DMA((2 * BACK + 1, ITEMS)),
+            pltpu.SemaphoreType.DMA((BACK + 1, ITEMS)),
             pltpu.SemaphoreType.DMA((3, PIECES)),
             pltpu.SemaphoreType.DMA((3, PIECES)),
             pltpu.SemaphoreType.DMA((PIECES,)),

time: 30.1 us -> 29.9 us (level); the launches traced: 29.6 us -> 29.8 us
  no operation moved by 1% of the time
where the time goes in v3:
time: 29.9 us; the launch traced here: 29.8 us
  Pallas kernels  28.9 us (97%)
  local copies, waits for them, and re-layouts  0.97 us (3%)
    pallas_call x1, Pallas kernels, body(): pl.pallas_call(kernel, name='attend', out_shape=pltpu.VMEM((BLOCK, 4 * GR...  28.9 us
    unnamed x1, local copies, waits for them, and re-layouts  0.97 us

profile of v3, /device:TPU:224, one launch (start us, length us, event | category | flops | bytes accessed | tf_op | source)
XLA Modules:
  0.0 29.8 jit_solution(17432075908953866562)
XLA Ops:
  0.0 28.9 %attend.1 = bf16[64,8192]{1,0:T(8,128)(2,1)S(1)} custom-call(bf16[4096,128]{1,0:T(8,128)(2,1)} %bitcast.4, bf16[256,128]{1,0:T(8,128)(2,1)} %bitcast.5, bf16[256,128]{1,0:T(8,128)(2,1)} %bitcast.6, s32[2,128]{1,0:T(2,128)} %bitcast.7), custom_call_target="tpu_custom_call" | custom-call | flops 2147483648 | bytes 4194304 | tf_op jit(solution)/shard_map/attend/pallas_call | solution.py:310
  28.9 1.0 %copy.6 = bf16[64,8192]{1,0:T(8,128)(2,1)} copy(bf16[64,8192]{1,0:T(8,128)(2,1)S(1)} %attend.1) | data formatting | bytes 2097152

commit v4 on v3

--- a/solution.py
+++ b/solution.py
@@ -14,9 +14,8 @@
 DIRECT = ([(1, 3), (2, 2), (2, 3), (3, 1)], [(1, 3), (2, 2), (2, 3), (3, 1)])
 PASSED = [[flow for flow in CROSS if flow not in straight] for straight in DIRECT]
 SHARD = 256
-CUTS = 1
-CUT = SHARD // CUTS
-ITEMS = 1 + 2 * CUTS
+LANDED = SHARD + 16
+ITEMS = 2
 GROUP = 16
 WIDTH = 128
 KEYS = (BACK + 1) * SHARD
@@ -33,7 +32,7 @@
 
 def kernel(
     q_hbm, k_hbm, v_hbm, ids_hbm, out_hbm,
-    q_buf, k_buf, v_buf, id_buf, vt_buf, k_pass, v_pass, id_pass, pick, bias, stage, turned,
+    q_buf, k_buf, v_buf, own_ids, vt_buf, k_pass, v_pass, pick, bias, stage, turned,
     load_sem, kv_send, kv_recv, out_send, out_recv, own_sem,
 ):
     ctx = lax.axis_index("ctx")
@@ -73,18 +72,18 @@
         return 2 * x + c
 
     barrier = pltpu.get_barrier_semaphore()
-    for by in range(1, BACK + 1):
-
-        @pl.when(reached[by])
-        def _():
-            pl.semaphore_signal(barrier, inc=1, device_id=(ctx - by, kvh), device_id_type=MESH)
-
-        @pl.when(fed[by])
-        def _():
-            pl.semaphore_signal(barrier, inc=1, device_id=(ctx - by + RING, kvh), device_id_type=MESH)
-
     for step in range(3):
         pl.semaphore_signal(barrier, inc=1, device_id=(ctx, owner(step)), device_id_type=MESH)
+
+    for by in range(1, BACK + 1):
+
+        @pl.when(reached[by])
+        def _():
+            pl.semaphore_signal(barrier, inc=1, device_id=(ctx - by, kvh), device_id_type=MESH)
+
+        @pl.when(fed[by])
+        def _():
+            pl.semaphore_signal(barrier, inc=1, device_id=(ctx - by + RING, kvh), device_id_type=MESH)
 
     @pl.when(takes)
     def _():
@@ -92,14 +91,19 @@
 
     own = BACK * SHARD
     loads = [
-        pltpu.make_async_copy(ids_hbm, id_buf.at[BACK], load_sem.at[0]),
+        pltpu.make_async_copy(ids_hbm, own_ids, load_sem.at[0]),
         pltpu.make_async_copy(k_hbm, k_buf.at[pl.ds(own, SHARD)], load_sem.at[1]),
-        pltpu.make_async_copy(v_hbm, v_buf.at[pl.ds(own, SHARD)], load_sem.at[2]),
+        pltpu.make_async_copy(v_hbm, v_buf.at[BACK, pl.ds(0, SHARD)], load_sem.at[2]),
         pltpu.make_async_copy(q_hbm, q_buf, load_sem.at[3]),
     ]
     for load in loads:
         load.start()
 
+    for load in loads[:3]:
+        load.wait()
+    ids = jnp.concatenate([own_ids[...].astype(jnp.float32), jnp.zeros((14, WIDTH), jnp.float32)], axis=0)
+    v_buf[BACK, SHARD:, :] = ids.astype(jnp.bfloat16)
+
     sent_to = [gives, *straight.values(), *onward.values()]
     pl.semaphore_wait(barrier, 3 + sum(to.astype(jnp.int32) for to in sent_to))
 
@@ -108,13 +112,11 @@
 
     def part(i, to):
         if isinstance(to, int) and to == BACK + 1:
-            return id_pass if i == 0 else (k_pass, v_pass)[(i - 1) // CUTS].at[pl.ds((i - 1) % CUTS * CUT, CUT)]
-        if i == 0:
-            return id_buf.at[to]
-        return (k_buf, v_buf)[(i - 1) // CUTS].at[part_rows(to, (i - 1) % CUTS * CUT, CUT)]
+            return (v_pass, k_pass)[i]
+        return v_buf.at[to] if i == 0 else k_buf.at[part_rows(to)]
 
     def move(i, to, target, passed):
-        src = ids_hbm if i == 0 else (k_hbm, v_hbm)[(i - 1) // CUTS].at[pl.ds((i - 1) % CUTS * CUT, CUT)]
+        src = part(i, BACK)
         slot = BACK if isinstance(to, int) and to > BACK else to
         if passed:
             src = part(i, BACK + 1)
@@ -146,30 +148,30 @@
         @pl.when(ctx < by)
         def _():
             rows = pl.ds((BACK - by) * SHARD, SHARD)
-            id_buf[BACK - by] = jnp.full((2, WIDTH), -1, jnp.int32)
             k_buf[rows] = jnp.zeros((SHARD, WIDTH), jnp.bfloat16)
-            v_buf[rows] = jnp.zeros((SHARD, WIDTH), jnp.bfloat16)
+            v_buf[BACK - by, :SHARD, :] = jnp.zeros((SHARD, WIDTH), jnp.bfloat16)
+            v_buf[BACK - by, SHARD:, :] = jnp.full((16, WIDTH), -1, jnp.bfloat16)
 
     token = lax.broadcasted_iota(jnp.int32, (SHARD // 2 * GROUP, WIDTH), 0) // GROUP
     lane = lax.broadcasted_iota(jnp.int32, (SHARD // 2 * GROUP, WIDTH), 1)
     pick[...] = jnp.where(token == lane, 1.0, 0.0).astype(jnp.bfloat16)
 
     def hide(to, causal=False):
+        key_ids = v_buf[to, SHARD:, :].astype(jnp.float32)
+        query_ids = v_buf[BACK, SHARD:, :].astype(jnp.float32)
         for r in range(2):
-            row = id_buf[to, r : r + 1, :].astype(jnp.float32)
-            column = jnp.broadcast_to(row, (WIDTH, WIDTH)).T
+            column = jnp.broadcast_to(key_ids[r : r + 1], (WIDTH, WIDTH)).T
             key_pos = lax.broadcasted_iota(jnp.int32, (WIDTH, WIDTH), 0) + r * WIDTH
             query_pos = lax.broadcasted_iota(jnp.int32, (WIDTH, WIDTH), 1)
             for half in range(2):
-                query = id_buf[BACK, half : half + 1, :].astype(jnp.float32)
-                seen = column == query
+                seen = column == query_ids[half : half + 1]
                 if causal:
                     seen = seen & (key_pos <= query_pos + half * WIDTH)
                 rows = part_rows(to, r * WIDTH, WIDTH)
                 bias[half, rows, :] = jnp.where(seen, 0.0, HIDE).astype(jnp.bfloat16)
 
     def turn(to):
-        vt_buf[:WIDTH, part_rows(to)] = v_buf[part_rows(to), :].T
+        vt_buf[:WIDTH, part_rows(to)] = v_buf[to, :SHARD, :].T
 
     def arrived(to, items):
         @pl.when(ctx >= BACK - to)
@@ -178,8 +180,7 @@
                 move(i, to, ctx, False).wait_recv()
 
     vt_buf[WIDTH:, :] = jnp.ones((16, KEYS), jnp.bfloat16)
-    for load in loads:
-        load.wait()
+    loads[3].wait()
     hide(BACK, causal=True)
     turn(BACK)
 
@@ -249,8 +250,8 @@
     early_sum = weighed(jnp.concatenate([vt_buf[:, part_rows(to)] for to in early], axis=1), score, early_top)
     arrived(late, [0])
     hide(late)
-    arrived(late, range(1, ITEMS))
     turn(late)
+    arrived(late, [1])
     score = scores(keys_of(late), queries)
     top = jnp.maximum(early_top, jnp.max(score, axis=0, keepdims=True))
     late_sum = weighed(vt_buf[:, part_rows(late)], score, top)
@@ -316,12 +317,11 @@
         scratch_shapes=[
             pltpu.VMEM((SHARD * GROUP, WIDTH), jnp.bfloat16),
             pltpu.VMEM((KEYS, WIDTH), jnp.bfloat16),
-            pltpu.VMEM((KEYS, WIDTH), jnp.bfloat16),
-            pltpu.VMEM((BACK + 1, 2, WIDTH), jnp.int32),
+            pltpu.VMEM((BACK + 1, LANDED, WIDTH), jnp.bfloat16),
+            pltpu.VMEM((2, WIDTH), jnp.int32),
             pltpu.VMEM((WIDTH + 16, KEYS), jnp.bfloat16),
             pltpu.VMEM((SHARD, WIDTH), jnp.bfloat16),
-            pltpu.VMEM((SHARD, WIDTH), jnp.bfloat16),
-            pltpu.VMEM((2, WIDTH), jnp.int32),
+            pltpu.VMEM((LANDED, WIDTH), jnp.bfloat16),
             pltpu.VMEM((SHARD // 2 * GROUP, WIDTH), jnp.bfloat16),
             pltpu.VMEM((2, KEYS, WIDTH), jnp.bfloat16),
             pltpu.VMEM((4, BLOCK, GROUP * WIDTH), jnp.bfloat16),

time: 29.9 us -> 29.8 us (level)
  no operation moved by 1% of the time
where the time goes in v4:
time: 29.8 us; the launch traced here: 29.7 us
  Pallas kernels  28.7 us (96%)
  local copies, waits for them, and re-layouts  0.97 us (3%)
    pallas_call x1, Pallas kernels, body(): pl.pallas_call(kernel, name='attend', out_shape=pltpu.VMEM((BLOCK, 4 * GR...  28.7 us
    unnamed x1, local copies, waits for them, and re-layouts  0.97 us

profile of v4, /device:TPU:224, one launch (start us, length us, event | category | flops | bytes accessed | tf_op | source)
XLA Modules:
  0.0 29.7 jit_solution(6562280408803298733)
XLA Ops:
  0.0 28.7 %attend.1 = bf16[64,8192]{1,0:T(8,128)(2,1)S(1)} custom-call(bf16[4096,128]{1,0:T(8,128)(2,1)} %bitcast.4, bf16[256,128]{1,0:T(8,128)(2,1)} %bitcast.5, bf16[256,128]{1,0:T(8,128)(2,1)} %bitcast.6, s32[2,128]{1,0:T(2,128)} %bitcast.7), custom_call_target="tpu_custom_call" | custom-call | flops 2147483648 | bytes 4194304 | tf_op jit(solution)/shard_map/attend/pallas_call | solution.py:311
  28.7 1.0 %copy.6 = bf16[64,8192]{1,0:T(8,128)(2,1)} copy(bf16[64,8192]{1,0:T(8,128)(2,1)S(1)} %attend.1) | data formatting | bytes 2097152

commit v5 on v4

--- a/solution.py
+++ b/solution.py
@@ -226,7 +226,7 @@
         return lax.dot_general(values, weight, PLAIN, preferred_element_type=jnp.float32)
 
     def finish(step, piece, summed):
-        turned[...] = (summed[:WIDTH] / summed[WIDTH : WIDTH + 1]).T
+        turned[...] = (summed[:WIDTH] * (1.0 / summed[WIDTH : WIDTH + 1])).T
         tokens = pl.ds(pl.multiple_of(piece * TILE, TILE), TILE)
         for head in range(GROUP):
             stage[step, tokens, head * WIDTH : (head + 1) * WIDTH] = turned[

time: 29.8 us -> 29.8 us (level)
  no operation moved by 1% of the time
where the time goes in v5:
time: 29.8 us; the launch traced here: 29.7 us
  Pallas kernels  28.7 us (96%)
  local copies, waits for them, and re-layouts  0.97 us (3%)
    pallas_call x1, Pallas kernels, body(): pl.pallas_call(kernel, name='attend', out_shape=pltpu.VMEM((BLOCK, 4 * GR...  28.7 us
    unnamed x1, local copies, waits for them, and re-layouts  0.97 us

profile of v5, /device:TPU:224, one launch (start us, length us, event | category | flops | bytes accessed | tf_op | source)
XLA Modules:
  0.0 29.7 jit_solution(11598051867669251253)
XLA Ops:
  0.0 28.7 %attend.1 = bf16[64,8192]{1,0:T(8,128)(2,1)S(1)} custom-call(bf16[4096,128]{1,0:T(8,128)(2,1)} %bitcast.4, bf16[256,128]{1,0:T(8,128)(2,1)} %bitcast.5, bf16[256,128]{1,0:T(8,128)(2,1)} %bitcast.6, s32[2,128]{1,0:T(2,128)} %bitcast.7), custom_call_target="tpu_custom_call" | custom-call | flops 2147483648 | bytes 4194304 | tf_op jit(solution)/shard_map/attend/pallas_call | solution.py:311
  28.7 1.0 %copy.6 = bf16[64,8192]{1,0:T(8,128)(2,1)} copy(bf16[64,8192]{1,0:T(8,128)(2,1)S(1)} %attend.1) | data formatting | bytes 2097152

commit v6 on v4

--- a/solution.py
+++ b/solution.py
@@ -11,7 +11,7 @@
 BACK = 3
 RING = 4
 CROSS = [(y, by) for y in range(RING) for by in range(1, BACK + 1) if y + by >= RING]
-DIRECT = ([(1, 3), (2, 2), (2, 3), (3, 1)], [(1, 3), (2, 2), (2, 3), (3, 1)])
+DIRECT = ([(1, 3), (2, 2), (2, 3), (3, 1)], [(1, 3), (2, 2), (2, 3), (3, 2)])
 PASSED = [[flow for flow in CROSS if flow not in straight] for straight in DIRECT]
 SHARD = 256
 LANDED = SHARD + 16

time: 29.8 us -> 30 us (level)
  the two profiles are of different devices: /device:TPU:224 before, /device:TPU:144 now
where the time goes in v6:
time: 30 us; the launch traced here: 29.9 us
  Pallas kernels  29 us (97%)
  local copies, waits for them, and re-layouts  0.97 us (3%)
    pallas_call x1, Pallas kernels, body(): pl.pallas_call(kernel, name='attend', out_shape=pltpu.VMEM((BLOCK, 4 * GR...  29 us
    unnamed x1, local copies, waits for them, and re-layouts  0.97 us

profile of v6, /device:TPU:144, one launch (start us, length us, event | category | flops | bytes accessed | tf_op | source)
XLA Modules:
  0.0 29.9 jit_solution(5090769956091351673)
XLA Ops:
  0.0 29.0 %attend.1 = bf16[64,8192]{1,0:T(8,128)(2,1)S(1)} custom-call(bf16[4096,128]{1,0:T(8,128)(2,1)} %bitcast.4, bf16[256,128]{1,0:T(8,128)(2,1)} %bitcast.5, bf16[256,128]{1,0:T(8,128)(2,1)} %bitcast.6, s32[2,128]{1,0:T(2,128)} %bitcast.7), custom_call_target="tpu_custom_call" | custom-call | flops 2147483648 | bytes 4194304 | tf_op jit(solution)/shard_map/attend/pallas_call | solution.py:311
  29.0 1.0 %copy.6 = bf16[64,8192]{1,0:T(8,128)(2,1)} copy(bf16[64,8192]{1,0:T(8,128)(2,1)S(1)} %attend.1) | data formatting | bytes 2097152
